TPU v7x, 32 devices: a whole 2x2x4 slice. The times are simulated.
32 devices in a mesh: member: 2 (over y), band: 16 (over z, x, core).
Axes of the slice: x: 2, y: 2, z: 4, core: 2. Of those that a mesh axis runs over, the one named last changes fastest.
Arguments:
- grid_latent: bfloat16 [16384, 512], P(('member', 'band')), parts along dimension 0, may hold values from -6 to 6
- mesh_latent: bfloat16 [10240, 512], P(('member', 'band')), parts along dimension 0, may hold values from -6 to 6
- g2m_latent: bfloat16 [24576, 512], P(('member', 'band')), parts along dimension 0, may hold values from -6 to 6
- edge_latent: bfloat16 [32768, 512], P(('member', 'band')), parts along dimension 0, may hold values from -6 to 6
- cotangent: bfloat16 [10240, 512], P(('member', 'band')), parts along dimension 0, may hold values from -8 to 8
- grid_send: int32 [16, 32], P('band'), may hold values from 0 to 511
- g2m_sender: int32 [12288], P('band'), may hold values from 0 to 543
- g2m_receiver: int32 [12288], P('band'), may hold values from 0 to 319
- node_send: int32 [16, 32], P('band'), may hold values from 0 to 319
- edge_sender: int32 [16384], P('band'), may hold values from 0 to 351
- edge_receiver: int32 [16384], P('band'), may hold values from 0 to 319
- edge_count: int32 [16], P('band'), may hold values from 1 to 1023, as said below
- enc_edge_in: bfloat16 [1536, 512], replicated, may hold values from -0.15625 to 0.15625
- enc_edge_out: bfloat16 [512, 512], replicated, may hold values from -0.25 to 0.25
- enc_node_in: bfloat16 [1024, 512], replicated, may hold values from -0.1875 to 0.1875
- enc_node_out: bfloat16 [512, 512], replicated, may hold values from -0.25 to 0.25
- proc_edge_in: bfloat16 [1536, 512], replicated, may hold values from -0.15625 to 0.15625
- proc_edge_out: bfloat16 [512, 512], replicated, may hold values from -0.25 to 0.25
- proc_node_in: bfloat16 [1024, 512], replicated, may hold values from -0.1875 to 0.1875
- proc_node_out: bfloat16 [512, 512], replicated, may hold values from -0.25 to 0.25
- norm_gains: float32 [4, 512], replicated, may hold values from 0.5 to 1.5
- norm_biases: float32 [4, 512], replicated, may hold values from -0.5 to 0.5
Outputs:
- mesh_out: bfloat16 [10240, 512], P(('member', 'band')), parts along dimension 0
- grad_mesh: float32 [10240, 512], P(('member', 'band')), parts along dimension 0
- grad_edge_in: float32 [3072, 512], P('member', 'band'), parts along dimension 0
- grad_edge_out: float32 [1024, 512], P('member', 'band'), parts along dimension 0
- grad_node_in: float32 [2048, 512], P('member', 'band'), parts along dimension 0
- grad_node_out: float32 [1024, 512], P('member', 'band'), parts along dimension 0
There are 2 independent parts, one for each index of `member`. A program takes and returns all parts, laid end to end along the dimension named above; an argument that names none is the same for every part. Nothing has to cross between parts.
Inputs may be any that keep to these rules, and one draw needn't show every extreme that they name: Device i's live mesh edges are its slots 0 to edge_count[i] - 1. For i < 8, devices i and i + 8 together hold at most 1024 live edges, and exactly that many in at least one such pair.
All inputs are finite; a program needn't handle non-finite values.
Results may differ from a plain program's by a relative error of at most 0.015.
Values may be sent and summed in bfloat16 or wider, within the bound.
A program may use at most 128 MiB of HBM per device.

v0:
```python
import jax
import jax.numpy as jnp
from jax import lax
from jax.sharding import PartitionSpec as P

EPS = 1e-05


def layer_norm(linear, gain_row, bias_row):
    average = jnp.mean(linear, axis=-1, keepdims=True)
    centred = linear - average
    inverse = lax.rsqrt(jnp.mean(centred * centred, axis=-1, keepdims=True) + EPS)
    return centred * inverse * gain_row + bias_row


def norm_back(linear, gain_row, upstream):
    average = jnp.mean(linear, axis=-1, keepdims=True)
    centred = linear - average
    inverse = lax.rsqrt(jnp.mean(centred * centred, axis=-1, keepdims=True) + EPS)
    normed = centred * inverse
    scaled = upstream * gain_row
    return inverse * (
        scaled
        - jnp.mean(scaled, axis=-1, keepdims=True)
        - normed * jnp.mean(scaled * normed, axis=-1, keepdims=True)
    )


def silu_slope(preact):
    sigmoid_val = jax.nn.sigmoid(preact)
    return sigmoid_val * (1.0 + preact * (1.0 - sigmoid_val))


def dense_pass(inputs, weight_in, weight_out, gain_row, bias_row):
    preact = jnp.dot(inputs, weight_in, preferred_element_type=jnp.float32)
    hidden = jax.nn.silu(preact).astype(jnp.bfloat16)
    linear = jnp.dot(hidden, weight_out, preferred_element_type=jnp.float32)
    return (preact, hidden, linear, layer_norm(linear, gain_row, bias_row))


def one_hot(indices, rows_total):
    return (indices[None, :] == jnp.arange(rows_total, dtype=jnp.int32)[:, None]).astype(
        jnp.bfloat16
    )


def on_device(
    grid_latent,
    mesh_latent,
    g2m_latent,
    edge_latent,
    cotangent,
    grid_send,
    g2m_sender,
    g2m_receiver,
    node_send,
    edge_sender,
    edge_receiver,
    edge_count,
    enc_edge_in,
    enc_edge_out,
    enc_node_in,
    enc_node_out,
    proc_edge_in,
    proc_edge_out,
    proc_node_in,
    proc_node_out,
    norm_gains,
    norm_biases,
):
    latent = mesh_latent.shape[1]
    node_rows = mesh_latent.shape[0]
    edge_cap = edge_latent.shape[0]
    devices = lax.axis_size("band")
    grid_outgoing = jnp.take(grid_latent, grid_send[0], axis=0)
    grid_arrived = lax.all_to_all(grid_outgoing, "band", split_axis=0, concat_axis=0, tiled=True)
    grid_table = jnp.concatenate([grid_latent, grid_arrived], axis=0)
    enc_inputs = jnp.concatenate(
        [
            jnp.take(grid_table, g2m_sender, axis=0),
            jnp.take(mesh_latent, g2m_receiver, axis=0),
            g2m_latent,
        ],
        axis=1,
    )
    enc_message = dense_pass(enc_inputs, enc_edge_in, enc_edge_out, norm_gains[0], norm_biases[0])[
        3
    ].astype(jnp.bfloat16)
    enc_sum = jnp.dot(
        one_hot(g2m_receiver, node_rows), enc_message, preferred_element_type=jnp.float32
    ).astype(jnp.bfloat16)
    enc_update = dense_pass(
        jnp.concatenate([mesh_latent, enc_sum], axis=1),
        enc_node_in,
        enc_node_out,
        norm_gains[1],
        norm_biases[1],
    )[3]
    encoded = (mesh_latent.astype(jnp.float32) + enc_update).astype(jnp.bfloat16)
    node_outgoing = jnp.take(encoded, node_send[0], axis=0)
    node_arrived = lax.all_to_all(node_outgoing, "band", split_axis=0, concat_axis=0, tiled=True)
    node_table = jnp.concatenate([encoded, node_arrived], axis=0)
    live_count = edge_count[0]
    slot_ids = jnp.arange(edge_cap, dtype=jnp.int32)
    live_mask = (slot_ids < live_count)[:, None]
    inputs = jnp.concatenate(
        [
            jnp.take(node_table, edge_sender, axis=0),
            jnp.take(encoded, edge_receiver, axis=0),
            edge_latent,
        ],
        axis=1,
    )
    preact, hidden, linear, normed = dense_pass(
        inputs, proc_edge_in, proc_edge_out, norm_gains[2], norm_biases[2]
    )
    work_message = (normed * live_mask.astype(jnp.float32)).astype(jnp.bfloat16)
    recv_hot = one_hot(edge_receiver, node_rows)
    proc_sum = jnp.dot(recv_hot, work_message, preferred_element_type=jnp.float32).astype(
        jnp.bfloat16
    )
    node_in = jnp.concatenate([encoded, proc_sum], axis=1)
    node_pre, node_hidden, node_linear, node_normed = dense_pass(
        node_in, proc_node_in, proc_node_out, norm_gains[3], norm_biases[3]
    )
    mesh_out = (encoded.astype(jnp.float32) + node_normed).astype(jnp.bfloat16)
    upstream = cotangent.astype(jnp.float32)
    node_lin_grad = norm_back(node_linear, norm_gains[3], upstream).astype(jnp.bfloat16)
    grad_node_out = jnp.dot(node_hidden.T, node_lin_grad, preferred_element_type=jnp.float32)
    node_pre_grad = (
        jnp.dot(node_lin_grad, proc_node_out.T, preferred_element_type=jnp.float32)
        * silu_slope(node_pre)
    ).astype(jnp.bfloat16)
    grad_node_in = jnp.dot(node_in.T, node_pre_grad, preferred_element_type=jnp.float32)
    node_in_grad = jnp.dot(node_pre_grad, proc_node_in.T, preferred_element_type=jnp.float32)
    sum_grad = node_in_grad[:, latent:].astype(jnp.bfloat16)
    msg_grad = jnp.take(sum_grad, edge_receiver, axis=0) * live_mask.astype(jnp.bfloat16)
    edge_lin_grad = norm_back(linear, norm_gains[2], msg_grad.astype(jnp.float32)).astype(
        jnp.bfloat16
    )
    grad_edge_out = jnp.dot(hidden.T, edge_lin_grad, preferred_element_type=jnp.float32)
    edge_pre_grad = (
        jnp.dot(edge_lin_grad, proc_edge_out.T, preferred_element_type=jnp.float32)
        * silu_slope(preact)
    ).astype(jnp.bfloat16)
    grad_edge_in = jnp.dot(inputs.T, edge_pre_grad, preferred_element_type=jnp.float32)
    work_input_grad = jnp.dot(
        edge_pre_grad, proc_edge_in[: 2 * latent].T, preferred_element_type=jnp.float32
    ).astype(jnp.bfloat16)
    table_grad = jnp.dot(
        one_hot(edge_sender, node_table.shape[0]),
        work_input_grad[:, :latent],
        preferred_element_type=jnp.float32,
    )
    recv_grad = jnp.dot(recv_hot, work_input_grad[:, latent:], preferred_element_type=jnp.float32)
    slot_grad = table_grad[node_rows:].astype(jnp.bfloat16)
    arrived_grad = lax.all_to_all(slot_grad, "band", split_axis=0, concat_axis=0, tiled=True)
    grad_mesh = (
        upstream
        + node_in_grad[:, :latent]
        + recv_grad
        + table_grad[:node_rows]
        + jnp.dot(
            one_hot(node_send[0], node_rows), arrived_grad, preferred_element_type=jnp.float32
        )
    )
    edge_scale = 1.0 / (edge_cap * devices) ** 0.5
    node_scale = 1.0 / (node_rows * devices) ** 0.5
    reduced = (
        lax.psum_scatter(grad_edge_in, "band", scatter_dimension=1, tiled=True),
        lax.psum_scatter(grad_edge_out, "band", scatter_dimension=1, tiled=True),
        lax.psum_scatter(grad_node_in, "band", scatter_dimension=1, tiled=True),
        lax.psum_scatter(grad_node_out, "band", scatter_dimension=1, tiled=True),
    )
    return (
        mesh_out,
        grad_mesh,
        reduced[0] * edge_scale,
        reduced[1] * edge_scale,
        reduced[2] * node_scale,
        reduced[3] * node_scale,
    )


def solution(mesh):
    placed = (
        P(("member", "band"), None),
        P(("member", "band"), None),
        P(("member", "band"), None),
        P(("member", "band"), None),
        P(("member", "band"), None),
        P("band", None),
        P("band"),
        P("band"),
        P("band", None),
        P("band"),
        P("band"),
        P("band"),
        P(),
        P(),
        P(),
        P(),
        P(),
        P(),
        P(),
        P(),
        P(),
        P(),
    )
    return jax.shard_map(
        on_device,
        mesh=mesh,
        in_specs=placed,
        out_specs=(
            P(("member", "band"), None),
            P(("member", "band"), None),
            P("member", "band"),
            P("member", "band"),
            P("member", "band"),
            P("member", "band"),
        ),
        check_vma=False,
    )
```

profile of v0, /device:TPU:0, one launch (start us, length us, event | category | flops | bytes accessed | tf_op | source)
XLA Modules:
  0.0 345.2 jit_solution(5832809643534543722)
XLA Ops:
  7.2 0.8 fusion.60
  8.5 1.3 reduce.6
  9.9 1.7 gather_fusion
  11.7 0.7 broadcast_select_fusion.5
  12.4 7.4 %all-to-all-start = ((bf16[16,2,512]{2,1,0:T(2,128)(2,1)}), bf16[16,2,512]{2,1,0:T(2,128)(2,1)S(1)}, u32[]{:S(2)}, u32[]{:S(2)}) async-start(bf16[16,2,512]{2,1,0:T(2,128)(2,1)} %broadcast_select_fusion.5), calls=%async_computation | async-start | bytes 65536 | tf_op jit(solution)/shard_map/all_to_all | solution.py:76
  19.8 0.7 compare_select_fusion.4
  20.5 0.7 compare_and_fusion.4
  21.9 0.7 compare_and_fusion.5
  23.2 1.3 reduce.7
  24.5 0.7 fusion.58
  25.2 0.7 compare_and_fusion.3
  25.9 0.7 fusion.59
  26.6 0.7 compare_and_fusion.2
  27.3 0.9 fusion.74
  28.2 0.9 fusion.75
  29.8 3.3 gather_fusion.2
  33.2 3.3 gather_fusion.1
  36.5 2.5 broadcast_select_fusion.2
  39.1 4.5 %fusion.76 = (f32[768]{0:T(1024)S(1)}, f32[768,512]{0,1:T(8,128)}) fusion(bf16[512,512]{1,0:T(8,128)(2,1)} %param.37, bf16[1536,512]{1,0:T(8,128)(2,1)S(1)} %copy-done, bf16[768,512]{1,0:T(8,128)(2,1)} %param.26, bf16[768,512]{1,0:T(8,128)(2,1)S(1)} %get-tuple-element.31, bf16[768,512]{1,0:T(8,128)(2,1)} %get-tuple-element.32), kind=kOutput, calls=%fused_computation.151 | convolution fusion | flops 1620049152 | bytes 6032384 | tf_op jit(solution)/shard_map/dot_general | solution.py:37
  43.5 1.6 multiply_reduce_fusion.2
  45.1 2.7 convolution_convert_fusion.1
  47.9 2.4 fusion.79
  51.4 0.7 broadcast_select_fusion.4
  52.1 6.0 %all-to-all-start.1 = ((bf16[16,2,512]{2,1,0:T(2,128)(2,1)}), bf16[16,2,512]{2,1,0:T(2,128)(2,1)S(1)}, u32[]{:S(2)}, u32[]{:S(2)}) async-start(bf16[16,2,512]{2,1,0:T(2,128)(2,1)} %broadcast_select_fusion.4), calls=%async_computation.1 | async-start | bytes 65536 | tf_op jit(solution)/shard_map/all_to_all | solution.py:101
  58.4 4.0 %gather_fusion.5 = bf16[1024,512]{1,0:T(8,128)(2,1)S(1)} fusion(bf16[320,512]{1,0:T(8,128)(2,1)S(1)} %add_convert_fusion.3, s32[1024]{0:T(1024)S(1)} %fusion.59), kind=kCustom, calls=%fused_computation.clone | custom fusion | bytes 2101248 | tf_op jit(solution)/shard_map/jit(_take)/gather | solution.py:109
  62.3 1.2 broadcast_select_fusion
  63.6 1.2 all-to-all-done.1
  64.8 4.0 %gather_fusion.4 = bf16[1024,512]{1,0:T(8,128)(2,1)S(1)} fusion(bf16[352,512]{1,0:T(8,128)(2,1)S(1)} %pad_maximum_fusion.7, s32[1024]{0:T(1024)S(1)} %fusion.58), kind=kCustom, calls=%fused_computation.6 | custom fusion | bytes 2101248 | tf_op jit(solution)/shard_map/jit(_take)/gather | solution.py:108
  69.0 1.0 copy-done.10
  70.4 5.0 %multiply_convert_fusion.3 = (bf16[1024,512]{1,0:T(8,128)(2,1)S(1)}, f32[1024,512]{1,0:T(8,128)}) fusion(bf16[1536,512]{1,0:T(8,128)(2,1)} %param.40, bf16[1024,512]{1,0:T(8,128)(2,1)S(1)} %copy-done.28, bf16[1024,512]{1,0:T(8,128)(2,1)S(1)} %copy-done.10, bf16[1024,512]{1,0:T(8,128)(2,1)S(1)} %broadcast_select_fusion.1), kind=kOutput, calls=%fused_computation.21 | convolution fusion | flops 1622671360 | bytes 7864320 | tf_op jit(solution)/shard_map/dot_general | solution.py:35
  75.4 0.8 fusion.82
  76.5 0.8 fusion.15
  80.8 1.1 fusion.38
  81.9 1.6 fusion.72
  83.5 1.7 fusion.14
  85.9 1.8 fusion.84
  87.7 1.2 copy-done.4
  88.9 5.1 %gather_fusion.6 = bf16[1024,512]{1,0:T(8,128)(2,1)} fusion(bf16[320,512]{1,0:T(8,128)(2,1)S(1)} %slice.94, s32[1024]{0:T(1024)S(1)} %fusion.59), kind=kCustom, calls=%fused_computation.1.clone | custom fusion | bytes 2101248 | tf_op jit(solution)/shard_map/jit(_take)/gather | solution.py:137
  94.0 1.5 copy.29
  95.5 2.4 fusion.6
  98.0 0.8 multiply_convert_fusion.1
  98.7 1.0 copy-done.17
  99.7 1.7 fusion.85
  101.5 2.1 fusion.52
  103.9 0.9 copy-done.18
  104.9 3.1 multiply_convert_fusion
  108.0 1.0 copy-done.32
  109.0 3.5 %fusion.10 = f32[1536,512]{0,1:T(8,128)} fusion(bf16[1024,512]{1,0:T(8,128)(2,1)S(1)} %multiply_convert_fusion, bf16[1024,512]{1,0:T(8,128)(2,1)S(1)} %copy-done.29, bf16[1024,512]{1,0:T(8,128)(2,1)S(1)} %copy-done.11, bf16[1024,512]{1,0:T(8,128)(2,1)S(1)} %copy-done.13), kind=kOutput, calls=%fused_computation.33 | convolution fusion | flops 1620049920 | bytes 7340032 | tf_op jit(solution)/shard_map/dot_general | solution.py:146
  112.5 1.2 copy-done.33
  113.7 2.5 convolution_convert_fusion
  116.3 1.3 copy-done.20
  118.1 0.9 copy-done.19
  119.6 4.8 %all-to-all-start.2 = ((bf16[16,2,512]{2,1,0:T(2,128)(2,1)}), bf16[16,2,512]{2,1,0:T(2,128)(2,1)S(1)}, u32[]{:S(2)}, u32[]{:S(2)}) async-start(bf16[16,2,512]{2,1,0:T(2,128)(2,1)} %all_to_all.24), calls=%async_computation.2 | async-start | bytes 65536 | tf_op jit(solution)/shard_map/all_to_all | solution.py:157
  124.5 2.8 fusion.13
  127.2 3.9 %all-to-all-done.2 = bf16[16,2,512]{2,1,0:T(2,128)(2,1)S(1)} async-done(((bf16[16,2,512]{2,1,0:T(2,128)(2,1)}), bf16[16,2,512]{2,1,0:T(2,128)(2,1)S(1)}, u32[]{:S(2)}, u32[]{:S(2)}) %all-to-all-start.2) | async-done | bytes 32800 | tf_op jit(solution)/shard_map/all_to_all | solution.py:157
  131.1 2.1 convolution_add_fusion
  133.3 9.6 %reduce-scatter.11.cloned.1.call-done = f32[512,32]{0,1:T(8,128)} async-done(((f32[512,512]{0,1:T(8,128)}), f32[512,32]{0,1:T(8,128)}) %reduce-scatter.11.cloned.1.call-update) | async-done | bytes 65552 | tf_op jit(solution)/shard_map/reduce_scatter | solution.py:173
  142.9 1.5 broadcast_multiply_fusion.2
  144.3 59.0 %reduce-scatter.7.cloned.1.call-done = f32[512,32]{0,1:T(8,128)} async-done(((f32[512,512]{0,1:T(8,128)}), f32[512,32]{0,1:T(8,128)}) %reduce-scatter.7.cloned.1.call-update) | async-done | bytes 65552 | tf_op jit(solution)/shard_map/reduce_scatter | solution.py:171
  203.3 1.5 broadcast_multiply_fusion.3
  204.8 62.9 %reduce-scatter.9.cloned.1.call-done = f32[1024,32]{0,1:T(8,128)} async-done(((f32[1024,512]{0,1:T(8,128)}), f32[1024,32]{0,1:T(8,128)}) %reduce-scatter.9.cloned.1.call-update) | async-done | bytes 131088 | tf_op jit(solution)/shard_map/reduce_scatter | solution.py:172
  267.7 1.6 broadcast_multiply_fusion.1
  269.3 67.8 %reduce-scatter.5.cloned.1.call-done = f32[1536,32]{0,1:T(8,128)} async-done(((f32[1536,512]{0,1:T(8,128)}), f32[1536,32]{0,1:T(8,128)}) %reduce-scatter.5.cloned.1.call-update) | async-done | bytes 196624 | tf_op jit(solution)/shard_map/reduce_scatter | solution.py:170
  337.0 1.6 broadcast_multiply_fusion
  (113 shorter events, 10.2 us)
Async XLA Ops:
  7.2 31.9 %copy-start = (bf16[1536,512]{1,0:T(8,128)(2,1)S(1)}, bf16[1536,512]{1,0:T(8,128)(2,1)}, u32[]{:S(2)}) copy-start(bf16[1536,512]{1,0:T(8,128)(2,1)} %param.36) | copy-start | bytes 4718596
  7.2 22.6 %copy-start.1 = (bf16[320,512]{1,0:T(8,128)(2,1)S(1)}, bf16[320,512]{1,0:T(8,128)(2,1)}, u32[]{:S(2)}) copy-start(bf16[320,512]{1,0:T(8,128)(2,1)} %param.25) | copy-start | bytes 983044
  12.4 20.7 %all-to-all-start = ((bf16[16,2,512]{2,1,0:T(2,128)(2,1)}), bf16[16,2,512]{2,1,0:T(2,128)(2,1)S(1)}, u32[]{:S(2)}, u32[]{:S(2)}) async-start(bf16[16,2,512]{2,1,0:T(2,128)(2,1)} %broadcast_select_fusion.5), calls=%async_computation | async-start | bytes 65536 | tf_op jit(solution)/shard_map/all_to_all | solution.py:76
  29.8 3.4 copy-start.9
  39.0 6.1 %copy-start.25 = (s32[768]{0:T(1024)S(1)}, s32[768]{0:T(1024)}, u32[]{:S(2)}) copy-start(s32[768]{0:T(1024)} %param.31) | copy-start | bytes 9220
  52.1 12.7 %all-to-all-start.1 = ((bf16[16,2,512]{2,1,0:T(2,128)(2,1)}), bf16[16,2,512]{2,1,0:T(2,128)(2,1)S(1)}, u32[]{:S(2)}, u32[]{:S(2)}) async-start(bf16[16,2,512]{2,1,0:T(2,128)(2,1)} %broadcast_select_fusion.4), calls=%async_computation.1 | async-start | bytes 65536 | tf_op jit(solution)/shard_map/all_to_all | solution.py:101
  58.1 84.7 %reduce-scatter.11.cloned.1.call-start = ((), (), s32[]{:S(2)}) async-start(), calls=%async_computation.10 | async-start | bytes 1114112 | tf_op jit(solution)/shard_map/reduce_scatter | solution.py:173
  68.8 1.2 copy-start.10
  68.8 1.5 copy-start.28
  70.4 5.0 %copy-start.12 = (bf16[1024,512]{1,0:T(8,128)(2,1)}, bf16[1024,512]{1,0:T(8,128)(2,1)S(1)}, u32[]{:S(2)}) copy-start(bf16[1024,512]{1,0:T(8,128)(2,1)S(1)} %broadcast_select_fusion.1) | copy-start | bytes 3145732
  70.4 5.0 %copy-start.21 = (bf16[512,512]{1,0:T(8,128)(2,1)S(1)}, bf16[512,512]{1,0:T(8,128)(2,1)}, u32[]{:S(2)}) copy-start(bf16[512,512]{1,0:T(8,128)(2,1)} %param.41) | copy-start | bytes 1572868
  75.4 1.1 copy-start.15
  75.4 1.1 copy-start.24
  76.2 1.3 copy-start.2
  76.5 1.6 copy-start.14
  78.2 1.6 copy-start.22
  78.2 1.2 copy-start.30
  79.3 2.6 copy-start.31
  79.3 1.2 copy-start.6
  85.2 0.7 copy-start.7
  85.3 118.0 %reduce-scatter.7.cloned.1.call-start = ((), (), s32[]{:S(2)}) async-start(), calls=%async_computation.8 | async-start | bytes 1114112 | tf_op jit(solution)/shard_map/reduce_scatter | solution.py:171
  87.7 1.2 copy-start.4
  95.5 2.5 copy-start.3
  98.0 1.8 copy-start.16
  98.7 1.0 copy-start.17
  99.7 1.8 copy-start.8
  99.7 1.8 copy-start.23
  101.5 166.2 %reduce-scatter.9.cloned.1.call-start = ((), (), s32[]{:S(2)}) async-start(), calls=%async_computation.9 | async-start | bytes 2228224 | tf_op jit(solution)/shard_map/reduce_scatter | solution.py:172
  103.6 1.2 copy-start.18
  103.7 233.4 %reduce-scatter.5.cloned.1.call-start = ((), (), s32[]{:S(2)}) async-start(), calls=%async_computation.7 | async-start | bytes 3342336 | tf_op jit(solution)/shard_map/reduce_scatter | solution.py:170
  104.9 4.1 %copy-start.11 = (bf16[1024,512]{1,0:T(8,128)(2,1)S(1)}, bf16[1024,512]{1,0:T(8,128)(2,1)}, u32[]{:S(2)}) copy-start(bf16[1024,512]{1,0:T(8,128)(2,1)} %broadcast_select_fusion) | copy-start | bytes 3145732
  104.9 4.1 %copy-start.13 = (bf16[1024,512]{1,0:T(8,128)(2,1)S(1)}, bf16[1024,512]{1,0:T(8,128)(2,1)}, u32[]{:S(2)}) copy-start(bf16[1024,512]{1,0:T(8,128)(2,1)} %copy-done.12) | copy-start | bytes 3145732
  104.9 4.1 %copy-start.29 = (bf16[1024,512]{1,0:T(8,128)(2,1)S(1)}, bf16[1024,512]{1,0:T(8,128)(2,1)}, u32[]{:S(2)}) copy-start(bf16[1024,512]{1,0:T(8,128)(2,1)} %param.27) | copy-start | bytes 3145732
  108.0 1.0 copy-start.32
  112.5 1.2 copy-start.33
  113.7 3.9 %copy-start.26 = (s32[1024]{0:T(1024)S(1)}, s32[1024]{0:T(1024)}, u32[]{:S(2)}) copy-start(s32[1024]{0:T(1024)} %param.33) | copy-start | bytes 12292
  116.2 1.3 copy-start.20
  117.6 6.9 %copy-start.5 = (f32[320,1024]{1,0:T(8,128)S(1)}, f32[320,1024]{1,0:T(8,128)}, u32[]{:S(2)}) copy-start(f32[320,1024]{1,0:T(8,128)} %copy-done.4) | copy-start | bytes 3932164
  118.1 0.9 copy-start.19
  119.0 12.1 %copy-start.27 = (s32[1,32]{1,0:T(1,128)S(1)}, s32[1,32]{1,0:T(1,128)}, u32[]{:S(2)}) copy-start(s32[1,32]{1,0:T(1,128)} %param.32) | copy-start | bytes 388
  119.6 11.4 %all-to-all-start.2 = ((bf16[16,2,512]{2,1,0:T(2,128)(2,1)}), bf16[16,2,512]{2,1,0:T(2,128)(2,1)S(1)}, u32[]{:S(2)}, u32[]{:S(2)}) async-start(bf16[16,2,512]{2,1,0:T(2,128)(2,1)} %all_to_all.24), calls=%async_computation.2 | async-start | bytes 65536 | tf_op jit(solution)/shard_map/all_to_all | solution.py:157
Sparse Core Ops, SparseCore 0:
  85.4 57.4 reduce-scatter.10
  146.9 56.3 reduce-scatter.6
  207.0 60.6 reduce-scatter.8
  271.8 65.1 reduce-scatter.4
where the time goes:
time: 347 us; the launch traced here: 345 us
  waiting for transfers between devices  204 us (59%)
  matrix products  40.7 us (12%)
  local copies, waits for them, and re-layouts  38 us (11%)
  other arithmetic  28.4 us (8%)
  starting transfers between devices  18.7 us (5%)
  between operations  14.9 us (4%)
    reduce_scatter x1, waiting for transfers between devices, on_device(): lax.psum_scatter(grad_edge_in, 'band', scatter_dimension=1, tiled=True)  67.8 us
    reduce_scatter x1, waiting for transfers between devices, on_device(): lax.psum_scatter(grad_node_in, 'band', scatter_dimension=1, tiled=True)  62.9 us
    reduce_scatter x1, waiting for transfers between devices, on_device(): lax.psum_scatter(grad_edge_out, 'band', scatter_dimension=1, tiled=True)  59 us
    unnamed x69, local copies, waits for them, and re-layouts  11.9 us
    reduce_scatter x1, waiting for transfers between devices, on_device(): lax.psum_scatter(grad_node_out, 'band', scatter_dimension=1, tiled=True)  9.58 us
    dot_general x4, matrix products, dense_pass(): linear = jnp.dot(hidden, weight_out, preferred_element_type=jnp.float32)  8.08 us
    all_to_all x1, starting transfers between devices, on_device(): lax.all_to_all(grid_outgoing, 'band', split_axis=0, concat_axis=0, tiled=...  7.36 us
  transfers between devices with their start and end apart: 7, of which 6 were waited for; matrix products, arithmetic and copies ran while one was open for 15% of the time, Pallas kernels for 0%

commit v1 on v0

v1 whole, which is shorter than its diff:
```python
import functools

import jax
import jax.numpy as jnp
from jax import lax
from jax.experimental import pallas as pl
from jax.experimental.pallas import tpu as pltpu
from jax.sharding import PartitionSpec as P

EPS = 1e-05
F32 = jnp.float32
BF16 = jnp.bfloat16
UNITS = 7
LANE = 128


def round_up(value, step):
    return (value + step - 1) // step * step


def nn(a, b):
    return jnp.dot(a, b, preferred_element_type=F32)


def nt(a, b):
    return lax.dot_general(a, b, (((1,), (1,)), ((), ())), preferred_element_type=F32)


def tn(a, b):
    return lax.dot_general(a, b, (((0,), (0,)), ((), ())), preferred_element_type=F32)


def sigmoid(a):
    return 0.5 * jnp.tanh(0.5 * a) + 0.5


def silu_slope(a):
    s = sigmoid(a)
    return s * (1.0 + a * (1.0 - s))


def normalise(linear):
    centred = linear - jnp.mean(linear, axis=-1, keepdims=True)
    inverse = lax.rsqrt(jnp.mean(centred * centred, axis=-1, keepdims=True) + EPS)
    return centred * inverse, inverse


def norm_back(z, inverse, scaled):
    return inverse * (
        scaled
        - jnp.mean(scaled, axis=-1, keepdims=True)
        - z * jnp.mean(scaled * z, axis=-1, keepdims=True)
    )


def hot_rows(index_row, rows_total, first=0):
    edges = index_row.shape[1]
    ids = lax.broadcasted_iota(jnp.int32, (rows_total, edges), 0) + first
    return jnp.where(ids == index_row, 1.0, 0.0).astype(BF16)


def over_lanes(index_row):
    edges = index_row.shape[1]
    return jnp.transpose(jnp.broadcast_to(index_row.astype(F32), (LANE, edges)))


def hot_pair(sender_row, receiver_row, split, total):
    edges = sender_row.shape[1]
    ids = lax.broadcasted_iota(jnp.int32, (edges, LANE), 1).astype(F32)
    senders, receivers = over_lanes(sender_row), over_lanes(receiver_row)
    blocks = []
    for start in range(0, total, LANE):
        held = senders if start < split else receivers
        offset = start if start < split else start - split
        blocks.append(jnp.where(held == ids + float(offset), 1.0, 0.0).astype(BF16))
    return jnp.concatenate(blocks, axis=1)


def kernel(n, inside, sizes, *refs):
    (grid_rows, nodes, enc_edges, slots_total, lat, tile, halo, split_enc, total_enc, split_proc, total_proc) = sizes
    stages = n.bit_length() - 1
    refs = list(refs)
    hbm = refs[:13]
    (count_ref, gsend_col, nsend_col, nsend_row, g2m_s, g2m_r, edge_s, edge_r, gains, biases) = refs[13:23]
    mesh_out_ref, grad_mesh_ref, grads_ref = refs[23:26]
    vm = refs[26:39]
    (table_enc, table_proc, node_table, acc_node, pre_ref, z_ref, inv_ref, hid_ref, elg_ref, epg_ref,
     sum_ref, upd_ref, a_send, a_recv, in_sem, a_ssem, a_rsem) = refs[39:56]
    rest = refs[56:]
    if inside:
        full_ref, keep, send, recv, r_ssem, r_rsem = (
            rest[0], rest[1:1 + stages], rest[1 + stages:1 + 2 * stages], rest[1 + 2 * stages:1 + 3 * stages],
            rest[1 + 3 * stages], rest[2 + 3 * stages])
    else:
        full_ref = grads_ref
    me = lax.axis_index("band")

    barrier = pltpu.get_barrier_semaphore()

    def greet(step, carry):
        pl.semaphore_signal(barrier, inc=1, device_id={"band": lax.rem(me + step, n)}, device_id_type=pl.DeviceIdType.MESH)
        return carry

    copies = [pltpu.make_async_copy(hbm[i], vm[i], in_sem.at[i]) for i in range(13)]
    (GRID, MESH, G2M, EDGE, COT, EEI, EEO, ENI, ENO, PEI, PEO, PNI, PNO) = range(13)
    for i in (GRID, EEI, MESH, G2M, EEO, ENI, ENO, PEI, EDGE, PEO, PNI, PNO, COT):
        copies[i].start()
    lax.fori_loop(1, n, greet, 0)

    rows_block = halo * lat // LANE // n
    spread = lat // LANE

    def exchange_start(which, rows):
        for c in range(spread):
            a_send[which, pl.ds(c, halo, stride=spread), :] = rows[:, c * LANE:(c + 1) * LANE]
        own = pl.ds(pl.multiple_of(me * rows_block, rows_block), rows_block)
        a_recv[which, own, :] = a_send[which, own, :]

        def go(step, carry):
            peer = lax.rem(me + step, n)
            pltpu.make_async_remote_copy(
                src_ref=a_send.at[which, pl.ds(pl.multiple_of(peer * rows_block, rows_block), rows_block)],
                dst_ref=a_recv.at[which, own],
                send_sem=a_ssem.at[which],
                recv_sem=a_rsem.at[which],
                device_id={"band": peer},
                device_id_type=pl.DeviceIdType.MESH,
            ).start()
            return carry

        lax.fori_loop(1, n, go, 0)

    def exchange_wait(which):
        most = pl.ds(0, (n - 1) * rows_block)
        pltpu.make_async_copy(a_send.at[which, most], a_recv.at[which, most], a_rsem.at[which]).wait()
        pltpu.make_async_copy(a_send.at[which, most], a_recv.at[which, most], a_ssem.at[which]).wait()
        return jnp.concatenate([a_recv[which, pl.ds(c, halo, stride=spread), :] for c in range(spread)], axis=1).astype(BF16)

    block = lat // n
    if inside:
        bits = [lax.rem(lax.div(me, jnp.int32(1 << k)), jnp.int32(2)) for k in range(stages)]

    def remote(units, k):
        first, count = units
        return pltpu.make_async_remote_copy(
            src_ref=send[k].at[pl.ds(first, count)],
            dst_ref=recv[k].at[pl.ds(first, count)],
            send_sem=r_ssem.at[first, k],
            recv_sem=r_rsem.at[first, k],
            device_id={"band": me + (1 - 2 * bits[k]) * (1 << k)},
            device_id_type=pl.DeviceIdType.MESH,
        )

    def reduce_step(units, k):
        if not inside:
            return
        first, count = units
        us = pl.ds(first, count)

        def value(j):
            rows = pl.ds(pl.multiple_of(j * block, block), block)
            if k == 0:
                return full_ref[us, rows, :]
            return keep[k - 1][us, rows, :] + recv[k - 1][us, rows, :].astype(F32)

        if k > 0:
            remote(units, k - 1).wait_recv()
        if k == stages:
            grads_ref[us, :, :] = value(0)
            return
        for j in range(n >> (k + 1)):
            send[k][us, j * block:(j + 1) * block, :] = value(2 * j + 1 - bits[k]).astype(BF16)
        remote(units, k).start()
        for j in range(n >> (k + 1)):
            keep[k][us, j * block:(j + 1) * block, :] = value(2 * j + bits[k])

    NODE, EOUT, EA, EB = (0, 3), (3, 1), (6, 1), (4, 2)

    copies[GRID].wait()
    grid = vm[GRID]
    ids = lax.broadcasted_iota(jnp.int32, (halo, grid_rows), 1)
    outgoing = nn(jnp.where(ids == gsend_col[...], 1.0, 0.0).astype(BF16), grid[...])
    pl.semaphore_wait(barrier, n - 1)
    exchange_start(0, outgoing)
    copies[EEI].wait()
    copies[MESH].wait()
    eei = vm[EEI]
    mesh = vm[MESH]
    table_enc[0:grid_rows, :] = nn(grid[...], eei[0:lat, :]).astype(BF16)
    table_enc[split_enc:split_enc + nodes, :] = nn(mesh[...], eei[lat:2 * lat, :]).astype(BF16)
    if split_enc > grid_rows + halo:
        table_enc[grid_rows + halo:split_enc, :] = jnp.zeros((split_enc - grid_rows - halo, lat), BF16)
    if total_enc > split_enc + nodes:
        table_enc[split_enc + nodes:total_enc, :] = jnp.zeros((total_enc - split_enc - nodes, lat), BF16)
    if split_proc > nodes + halo:
        table_proc[nodes + halo:split_proc, :] = jnp.zeros((split_proc - nodes - halo, lat), BF16)
    if total_proc > split_proc + nodes:
        table_proc[split_proc + nodes:total_proc, :] = jnp.zeros((total_proc - split_proc - nodes, lat), BF16)
    copies[G2M].wait()
    copies[EEO].wait()
    copies[ENI].wait()
    acc_node[...] = jnp.zeros_like(acc_node)
    upd_ref[...] = nn(mesh[...], vm[ENI][0:lat, :])
    arrived = exchange_wait(0)
    table_enc[grid_rows:grid_rows + halo, :] = nn(arrived, eei[0:lat, :]).astype(BF16)

    def encode(t, carry):
        rows = pl.ds(pl.multiple_of(t * tile, tile), tile)
        receivers = g2m_r[t]
        pre = nn(hot_pair(g2m_s[t], receivers, split_enc, total_enc), table_enc[...])
        pre = pre + nn(vm[G2M][rows, :], eei[2 * lat:3 * lat, :])
        hidden = (pre * sigmoid(pre)).astype(BF16)
        z, _ = normalise(nn(hidden, vm[EEO][...]))
        message = (z * gains[0:1, :] + biases[0:1, :]).astype(BF16)
        acc_node[...] += nn(hot_rows(receivers, nodes), message)
        return carry

    lax.fori_loop(0, enc_edges // tile, encode, 0)
    copies[ENO].wait()
    pre = upd_ref[...] + nn(acc_node[...].astype(BF16), vm[ENI][lat:2 * lat, :])
    hidden = (pre * sigmoid(pre)).astype(BF16)
    z, _ = normalise(nn(hidden, vm[ENO][...]))
    encoded = (mesh[...].astype(F32) + z * gains[1:2, :] + biases[1:2, :]).astype(BF16)
    node_table[0:nodes, :] = encoded
    ids = lax.broadcasted_iota(jnp.int32, (halo, nodes), 1)
    exchange_start(1, nn(jnp.where(ids == nsend_col[...], 1.0, 0.0).astype(BF16), encoded))

    copies[PEI].wait()
    copies[EDGE].wait()
    copies[PEO].wait()
    copies[PNI].wait()
    pei, pni = vm[PEI], vm[PNI]
    table_proc[0:nodes, :] = nn(encoded, pei[0:lat, :]).astype(BF16)
    table_proc[split_proc:split_proc + nodes, :] = nn(encoded, pei[lat:2 * lat, :]).astype(BF16)
    upd_ref[...] = nn(encoded, pni[0:lat, :])

    def edge_part(t, carry):
        rows = pl.ds(pl.multiple_of(t * tile, tile), tile)
        pre_ref[rows, :] = nn(vm[EDGE][rows, :], pei[2 * lat:3 * lat, :])
        return carry

    lax.fori_loop(0, slots_total // tile, edge_part, 0)
    acc_node[...] = jnp.zeros_like(acc_node)
    arrived = exchange_wait(1)
    node_table[nodes:nodes + halo, :] = arrived
    table_proc[nodes:nodes + halo, :] = nn(arrived, pei[0:lat, :]).astype(BF16)
    count = count_ref[0]

    def live_rows(ref, t):
        slot = lax.broadcasted_iota(jnp.int32, (1, tile), 1) + t * tile
        return jnp.where(slot < count, ref[t], -1)

    def process(t, carry):
        rows = pl.ds(pl.multiple_of(t * tile, tile), tile)
        receivers = live_rows(edge_r, t)
        pre = pre_ref[rows, :] + nn(hot_pair(live_rows(edge_s, t), receivers, split_proc, total_proc), table_proc[...])
        pre_ref[rows, :] = pre
        hidden = (pre * sigmoid(pre)).astype(BF16)
        hid_ref[rows, :] = hidden
        z, inverse = normalise(nn(hidden, vm[PEO][...]))
        z_ref[rows, :] = z
        inv_ref[rows, :] = jnp.broadcast_to(inverse, (tile, LANE))
        message = (z * gains[2:3, :] + biases[2:3, :]).astype(BF16)
        acc_node[...] += nn(hot_rows(receivers, nodes), message)
        return carry

    lax.fori_loop(0, slots_total // tile, process, 0)

    proc_sum = acc_node[...].astype(BF16)
    copies[PNO].wait()
    copies[COT].wait()
    pno, cot = vm[PNO], vm[COT]
    pre = upd_ref[...] + nn(proc_sum, pni[lat:2 * lat, :])
    hidden = (pre * sigmoid(pre)).astype(BF16)
    z, inverse = normalise(nn(hidden, pno[...]))
    mesh_out_ref[...] = (encoded.astype(F32) + z * gains[3:4, :] + biases[3:4, :]).astype(BF16)
    lin_grad = norm_back(z, inverse, cot[...].astype(F32) * gains[3:4, :]).astype(BF16)
    pre_grad = (nt(lin_grad, pno[...]) * silu_slope(pre)).astype(BF16)
    full_ref[0, :, :] = tn(lin_grad, hidden)
    full_ref[1, :, :] = tn(pre_grad, encoded)
    full_ref[2, :, :] = tn(pre_grad, proc_sum)
    reduce_step(NODE, 0)
    sum_grad = nt(pre_grad, pni[lat:2 * lat, :]).astype(BF16)
    grad_mesh_ref[...] = cot[...].astype(F32) + nt(pre_grad, pni[0:lat, :])
    if split_proc + nodes < total_proc:
        table_proc[split_proc + nodes:total_proc, :] = jnp.zeros((total_proc - split_proc - nodes, lat), BF16)
    table_proc[split_proc:split_proc + nodes, :] = sum_grad
    sum_ref[...] = jnp.zeros_like(sum_ref)

    def edge_back(t, carry):
        rows = pl.ds(pl.multiple_of(t * tile, tile), tile)
        senders, receivers = live_rows(edge_s, t), live_rows(edge_r, t)
        held = over_lanes(receivers)
        ids = lax.broadcasted_iota(jnp.int32, (tile, LANE), 1).astype(F32)
        hot = jnp.concatenate(
            [jnp.where(held == ids + float(s), 1.0, 0.0).astype(BF16) for s in range(0, total_proc - split_proc, LANE)], axis=1)
        upstream = nn(hot, table_proc[split_proc:total_proc, :])
        grad = norm_back(z_ref[rows, :], inv_ref[rows, 0:1], upstream * gains[2:3, :]).astype(BF16)
        elg_ref[rows, :] = grad
        grad = (nt(grad, vm[PEO][...]) * silu_slope(pre_ref[rows, :])).astype(BF16)
        epg_ref[rows, :] = grad
        sum_ref[0:split_proc, :] += nn(hot_rows(senders, split_proc), grad)
        sum_ref[split_proc:split_proc + nodes, :] += nn(hot_rows(receivers, nodes), grad)
        return carry

    half = slots_total // tile // 2
    lax.fori_loop(0, half, edge_back, 0)
    reduce_step(NODE, 1)
    lax.fori_loop(half, slots_total // tile, edge_back, 0)
    reduce_step(NODE, 2)
    by_sender = sum_ref[0:nodes + halo, :].astype(BF16)
    by_receiver = sum_ref[split_proc:split_proc + nodes, :].astype(BF16)
    exchange_start(2, nt(by_sender[nodes:nodes + halo, :], pei[0:lat, :]))
    full_ref[3, :, :] = tn(elg_ref[...], hid_ref[...])
    reduce_step(EOUT, 0)
    full_ref[6, :, :] = tn(epg_ref[...], vm[EDGE][...])
    reduce_step(EA, 0)
    reduce_step(NODE, 3)
    reduce_step(EOUT, 1)
    full_ref[4, :, :] = tn(by_sender, node_table[...])
    full_ref[5, :, :] = tn(by_receiver, node_table[0:nodes, :])
    reduce_step(EB, 0)
    reduce_step(EA, 1)
    grad_mesh_ref[...] += nt(by_sender[0:nodes, :], pei[0:lat, :]) + nt(by_receiver, pei[lat:2 * lat, :])
    reduce_step(EB, 1)
    reduce_step(EOUT, 2)
    arrived = exchange_wait(2)
    grad_mesh_ref[...] += nn(hot_rows(nsend_row[...], nodes), arrived)
    reduce_step(NODE, 4)
    reduce_step(EA, 2)
    reduce_step(EOUT, 3)
    reduce_step(EB, 2)
    reduce_step(EA, 3)
    reduce_step(EOUT, 4)
    reduce_step(EB, 3)
    reduce_step(EA, 4)
    reduce_step(EB, 4)
    if inside:
        for units in (NODE, EOUT, EA, EB):
            for k in range(stages):
                remote(units, k).wait_send()


def on_device(n, *args):
    (grid_latent, mesh_latent, g2m_latent, edge_latent, cotangent, grid_send, g2m_sender, g2m_receiver, node_send,
     edge_sender, edge_receiver, edge_count, *weights) = args
    weights, (gains, biases) = weights[:8], weights[8:]
    lat = mesh_latent.shape[1]
    grid_rows, nodes = grid_latent.shape[0], mesh_latent.shape[0]
    enc_edges, slots_total = g2m_latent.shape[0], edge_latent.shape[0]
    halo = node_send.shape[1]
    tile = 256
    inside = n == 16
    split_enc = round_up(grid_rows + halo, LANE)
    split_proc = round_up(nodes + halo, LANE)
    total_enc = round_up(split_enc + nodes, LANE)
    total_proc = round_up(split_proc + nodes, LANE)
    sizes = (grid_rows, nodes, enc_edges, slots_total, lat, tile, halo, split_enc, total_enc, split_proc, total_proc)
    stages = n.bit_length() - 1
    large = [grid_latent, mesh_latent, g2m_latent, edge_latent, cotangent, *weights]
    small = [
        grid_send.reshape(halo, 1), node_send.reshape(halo, 1), node_send,
        g2m_sender.reshape(-1, 1, tile), g2m_receiver.reshape(-1, 1, tile),
        edge_sender.reshape(-1, 1, tile), edge_receiver.reshape(-1, 1, tile), gains, biases,
    ]
    in_vmem = pl.BlockSpec(memory_space=pltpu.VMEM)
    scratch = [pltpu.VMEM(a.shape, a.dtype) for a in large]
    scratch += [
        pltpu.VMEM((total_enc, lat), BF16),
        pltpu.VMEM((total_proc, lat), BF16),
        pltpu.VMEM((nodes + halo, lat), BF16),
        pltpu.VMEM((nodes, lat), F32),
        pltpu.VMEM((slots_total, lat), F32),
        pltpu.VMEM((slots_total, lat), F32),
        pltpu.VMEM((slots_total, LANE), F32),
        pltpu.VMEM((slots_total, lat), BF16),
        pltpu.VMEM((slots_total, lat), BF16),
        pltpu.VMEM((slots_total, lat), BF16),
        pltpu.VMEM((total_proc, lat), F32),
        pltpu.VMEM((nodes, lat), F32),
        pltpu.VMEM((3, halo * lat // LANE, LANE), F32),
        pltpu.VMEM((3, halo * lat // LANE, LANE), F32),
        pltpu.SemaphoreType.DMA((13,)),
        pltpu.SemaphoreType.DMA((3,)),
        pltpu.SemaphoreType.DMA((3,)),
    ]
    if inside:
        scratch += [pltpu.VMEM((UNITS, lat, lat), F32)]
        for dtype in (F32, BF16, BF16):
            scratch += [pltpu.VMEM((UNITS, lat >> (k + 1), lat), dtype) for k in range(stages)]
        scratch += [pltpu.SemaphoreType.DMA((UNITS, stages)), pltpu.SemaphoreType.DMA((UNITS, stages))]
    mesh_out, grad_mesh, grads = pl.pallas_call(
        functools.partial(kernel, n, inside, sizes),
        out_shape=(
            jax.ShapeDtypeStruct((nodes, lat), BF16),
            jax.ShapeDtypeStruct((nodes, lat), F32),
            jax.ShapeDtypeStruct((UNITS, lat // n if inside else lat, lat), F32),
        ),
        in_specs=[pl.BlockSpec(memory_space=pl.ANY)] * 13 + [pl.BlockSpec(memory_space=pltpu.SMEM)] + [in_vmem] * len(small),
        out_specs=(in_vmem, in_vmem, in_vmem),
        scratch_shapes=scratch,
        compiler_params=pltpu.CompilerParams(collective_id=0, has_side_effects=True, vmem_limit_bytes=60 * 1024 * 1024),
    )(*large, edge_count, *small)
    if not inside:
        grads = lax.psum_scatter(grads, "band", scatter_dimension=1, tiled=True)
    edge_scale = 1.0 / (slots_total * n) ** 0.5
    node_scale = 1.0 / (nodes * n) ** 0.5

    def shard(first, count, scale):
        return jnp.transpose(grads[first:first + count], (0, 2, 1)).reshape(count * lat, lat // n) * scale

    return (mesh_out, grad_mesh, shard(4, 3, edge_scale), shard(3, 1, edge_scale), shard(1, 2, node_scale), shard(0, 1, node_scale))


def solution(mesh):
    rows = P(("member", "band"), None)
    placed = (rows,) * 5 + (P("band", None), P("band"), P("band"), P("band", None), P("band"), P("band"), P("band")) + (P(),) * 10
    shard = P("member", "band")
    return jax.shard_map(
        functools.partial(on_device, mesh.shape["band"]),
        mesh=mesh,
        in_specs=placed,
        out_specs=(rows, rows, shard, shard, shard, shard),
        check_vma=False,
    )
```

time: 347 us -> 81.5 us (0.23)
  waiting for transfers between devices: 204 us -> 0 us
  Pallas kernels: 0 us -> 68.3 us
  matrix products: 40.7 us -> 0 us
  local copies, waits for them, and re-layouts: 38 us -> 8.15 us
  other arithmetic: 28.4 us -> 3.47 us
  starting transfers between devices: 18.7 us -> 0 us
  between operations: 14.9 us -> 1.31 us
    reduce_scatter x4 -> x0, waiting for transfers between devices: 199 us -> none  [the longest x1 67.8 us: on_device(): lax.psum_scatter(grad_edge_in, 'band', scatter_dimension=1, tiled=True)]
    pallas_call x0 -> x1, Pallas kernels: none -> 68.3 us  [on_device(): pl.pallas_call(functools.partial(kernel, n, inside, sizes), out_shape=(ja...]
    dot_general x19 -> x0, matrix products: 40.7 us -> none  [the longest x4 8.08 us: dense_pass(): linear = jnp.dot(hidden, weight_out, preferred_element_type=jnp.float32)]
    gather x10 -> x0, local copies, waits for them, and re-layouts: 23.5 us -> none  [the longest x2 6.57 us: on_device(): jnp.take(sum_grad, edge_receiver, axis=0) * live_mask.astype(jnp.bfloat16)]
    all_to_all x3 -> x0, starting transfers between devices: 18.2 us -> none  [the longest x1 7.36 us: on_device(): lax.all_to_all(grid_outgoing, 'band', split_axis=0, concat_axis=0, tiled=...]
    unnamed x69 -> x6, local copies, waits for them, and re-layouts: 11.9 us -> 1.57 us
    select_n x9 -> x0, other arithmetic: 8.18 us -> none  [the longest x2 3.19 us: on_device(): jnp.take(mesh_latent, g2m_receiver, axis=0)]
    reshape x0 -> x4, local copies, waits for them, and re-layouts: none -> 5.22 us  [the longest x1 1.34 us: on_device(): grid_send.reshape(halo, 1)]
  transfers between devices with their start and end apart: 7 -> 0, of which waited for: 6 -> 0; matrix products, arithmetic and copies ran while one was open for 15% -> 0% of each run, Pallas kernels for 0% -> 0%
where the time goes in v1:
time: 81.5 us; the launch traced here: 81.2 us
  Pallas kernels  68.3 us (84%)
  local copies, waits for them, and re-layouts  8.15 us (10%)
  other arithmetic  3.47 us (4%)
  between operations  1.31 us (2%)
    pallas_call x1, Pallas kernels, on_device(): pl.pallas_call(functools.partial(kernel, n, inside, sizes), out_shape=(ja...  68.3 us
    unnamed x2, other arithmetic  1.94 us

profile of v1, /device:TPU:0, one launch (start us, length us, event | category | flops | bytes accessed | tf_op | source)
XLA Modules:
  0.0 81.2 jit_solution(7946335953588485794)
XLA Ops:
  1.3 1.3 %reshape.44.refs_17_ = s32[3,1,256]{2,1,0:T(1,128)} reshape(s32[768]{0:T(1024)} %param.28) | data formatting | bytes 6144 | tf_op jit(solution)/shard_map/reshape | solution.py:363
  2.6 1.3 %reshape.45.refs_18_ = s32[3,1,256]{2,1,0:T(1,128)} reshape(s32[768]{0:T(1024)} %param.29) | data formatting | bytes 6144 | tf_op jit(solution)/shard_map/reshape | solution.py:363
  3.8 1.3 %copy.30.refs_14_ = s32[32,1]{1,0:T(8,128)} copy(s32[32,1]{0,1:T(1,128)} %bitcast.25) | data formatting | bytes 256 | tf_op jit(solution)/shard_map/reshape | solution.py:362
  5.2 1.3 %copy.31.refs_15_ = s32[32,1]{1,0:T(8,128)} copy(s32[32,1]{0,1:T(1,128)} %bitcast.24) | data formatting | bytes 256 | tf_op jit(solution)/shard_map/reshape | solution.py:362
  6.5 68.3 %shard_map.253 = (bf16[320,512]{1,0:T(8,128)(2,1)}, f32[320,512]{1,0:T(8,128)}, f32[7,32,512]{2,1,0:T(8,128)}) custom-call(bf16[512,512]{1,0:T(8,128)(2,1)} %refs_0_.1, bf16[320,512]{1,0:T(8,128)(2,1)} %refs_1_.1, bf16[768,512]{1,0:T(8,128)(2,1)} %refs_2_.1, bf16[1024,512]{1,0:T(8,128)(2,1)} %refs_3_.1, bf16[320,512]{1,0:T(8,128)(2,1)} %refs_4_.1, ...), custom_call_target="tpu_custom_call" | custom-call | tf_op jit(solution)/shard_map/pallas_call | solution.py:392
  74.8 0.0 copy-start.1
  74.8 0.0 copy-start
  74.8 1.0 %multiply_bitcast_fusion.1 = f32[2,4,8,512]{3,2,1,0:T(8,128)S(1)} fusion(f32[7,32,512]{2,1,0:T(8,128)} %get-tuple-element.11), kind=kLoop, calls=%fused_computation.1 | loop fusion | flops 32768 | bytes 262144
  75.8 0.7 copy.35
  76.5 1.5 %multiply_bitcast_fusion.2 = (f32[512,32]{0,1:T(8,128)}, f32[512,32]{0,1:T(8,128)}) fusion(f32[7,32,512]{2,1,0:T(8,128)} %get-tuple-element.11), kind=kLoop, calls=%fused_computation.2 | loop fusion | flops 32768 | bytes 262144 | tf_op jit(solution)/shard_map/mul | solution.py:410
  78.0 0.9 %multiply_bitcast_fusion = f32[3,4,8,512]{3,2,1,0:T(8,128)S(1)} fusion(f32[7,32,512]{2,1,0:T(8,128)} %get-tuple-element.11), kind=kLoop, calls=%fused_computation | loop fusion | flops 49152 | bytes 393216
  78.9 0.7 copy.34
  79.6 0.0 copy-done.1
  79.6 0.7 copy.39
  80.3 0.0 copy-done
  80.4 0.8 %copy.40 = f32[320,512]{1,0:T(8,128)} copy(f32[320,512]{1,0:T(8,128)S(1)} %copy-done) | data formatting | bytes 1310720
Async XLA Ops:
  74.8 4.9 %copy-start.1 = (bf16[320,512]{1,0:T(8,128)(2,1)S(1)}, bf16[320,512]{1,0:T(8,128)(2,1)}, u32[]{:S(2)}) copy-start(bf16[320,512]{1,0:T(8,128)(2,1)} %get-tuple-element.20) | copy-start | bytes 983044
  74.8 5.6 %copy-start = (f32[320,512]{1,0:T(8,128)S(1)}, f32[320,512]{1,0:T(8,128)}, u32[]{:S(2)}) copy-start(f32[320,512]{1,0:T(8,128)} %get-tuple-element.21) | copy-start | bytes 1966084

commit v2 on v1

--- a/solution.py
+++ b/solution.py
@@ -81,18 +81,19 @@
     stages = n.bit_length() - 1
     refs = list(refs)
     hbm = refs[:13]
-    (count_ref, gsend_col, nsend_col, nsend_row, g2m_s, g2m_r, edge_s, edge_r, gains, biases) = refs[13:23]
-    mesh_out_ref, grad_mesh_ref, grads_ref = refs[23:26]
-    vm = refs[26:39]
+    (count_ref, gsend_row, nsend_row, g2m_s, g2m_r, edge_s, edge_r, gains, biases) = refs[13:22]
+    mesh_out_ref, grad_mesh_ref = refs[22:24]
+    outs, refs = refs[24:28 if inside else 25], refs[28 if inside else 25:]
+    vm = refs[:13]
     (table_enc, table_proc, node_table, acc_node, pre_ref, z_ref, inv_ref, hid_ref, elg_ref, epg_ref,
-     sum_ref, upd_ref, a_send, a_recv, in_sem, a_ssem, a_rsem) = refs[39:56]
-    rest = refs[56:]
+     sum_ref, upd_ref, a_send, a_recv, in_sem, a_ssem, a_rsem) = refs[13:30]
+    rest = refs[30:]
     if inside:
         full_ref, keep, send, recv, r_ssem, r_rsem = (
             rest[0], rest[1:1 + stages], rest[1 + stages:1 + 2 * stages], rest[1 + 2 * stages:1 + 3 * stages],
             rest[1 + 3 * stages], rest[2 + 3 * stages])
     else:
-        full_ref = grads_ref
+        full_ref = outs[0]
     me = lax.axis_index("band")
 
     barrier = pltpu.get_barrier_semaphore()
@@ -110,9 +111,11 @@
     rows_block = halo * lat // LANE // n
     spread = lat // LANE
 
-    def exchange_start(which, rows):
+    def exchange_fill(which, rows):
         for c in range(spread):
             a_send[which, pl.ds(c, halo, stride=spread), :] = rows[:, c * LANE:(c + 1) * LANE]
+
+    def exchange_start(which):
         own = pl.ds(pl.multiple_of(me * rows_block, rows_block), rows_block)
         a_recv[which, own, :] = a_send[which, own, :]
 
@@ -141,20 +144,21 @@
         bits = [lax.rem(lax.div(me, jnp.int32(1 << k)), jnp.int32(2)) for k in range(stages)]
 
     def remote(units, k):
-        first, count = units
+        first, count, order, _ = units
+        bit = order[k]
         return pltpu.make_async_remote_copy(
             src_ref=send[k].at[pl.ds(first, count)],
             dst_ref=recv[k].at[pl.ds(first, count)],
             send_sem=r_ssem.at[first, k],
             recv_sem=r_rsem.at[first, k],
-            device_id={"band": me + (1 - 2 * bits[k]) * (1 << k)},
+            device_id={"band": me + (1 - 2 * bits[bit]) * (1 << bit)},
             device_id_type=pl.DeviceIdType.MESH,
         )
 
     def reduce_step(units, k):
         if not inside:
             return
-        first, count = units
+        first, count, order, place = units
         us = pl.ds(first, count)
 
         def value(j):
@@ -166,22 +170,36 @@
         if k > 0:
             remote(units, k - 1).wait_recv()
         if k == stages:
-            grads_ref[us, :, :] = value(0)
+            total = value(0)
+            for unit in range(count):
+                which, column, scale = place[unit]
+                outs[which][:, column * lat:(column + 1) * lat] = total[unit] * scale
             return
+        at = sorted(order[k:]).index(order[k])
+        bit = bits[order[k]]
+
+        def whole(j, chosen):
+            return ((j >> at) << (at + 1)) + (j & ((1 << at) - 1)) + chosen * (1 << at)
+
         for j in range(n >> (k + 1)):
-            send[k][us, j * block:(j + 1) * block, :] = value(2 * j + 1 - bits[k]).astype(BF16)
+            send[k][us, j * block:(j + 1) * block, :] = value(whole(j, 1 - bit)).astype(BF16)
         remote(units, k).start()
         for j in range(n >> (k + 1)):
-            keep[k][us, j * block:(j + 1) * block, :] = value(2 * j + bits[k])
-
-    NODE, EOUT, EA, EB = (0, 3), (3, 1), (6, 1), (4, 2)
+            keep[k][us, j * block:(j + 1) * block, :] = value(whole(j, bit))
+
+    low_first, high_first = (0, 1, 2, 3), (0, 2, 3, 1)
+    edge_scale = 1.0 / (slots_total * n) ** 0.5
+    node_scale = 1.0 / (nodes * n) ** 0.5
+    N0 = (0, 1, high_first, ((3, 0, node_scale),))
+    N12 = (1, 2, low_first, ((2, 0, node_scale), (2, 1, node_scale)))
+    EOUT = (3, 1, low_first, ((1, 0, edge_scale),))
+    E4 = (4, 1, low_first, ((0, 0, edge_scale),))
+    E5 = (5, 1, high_first, ((0, 1, edge_scale),))
+    E6 = (6, 1, low_first, ((0, 2, edge_scale),))
 
     copies[GRID].wait()
     grid = vm[GRID]
-    ids = lax.broadcasted_iota(jnp.int32, (halo, grid_rows), 1)
-    outgoing = nn(jnp.where(ids == gsend_col[...], 1.0, 0.0).astype(BF16), grid[...])
-    pl.semaphore_wait(barrier, n - 1)
-    exchange_start(0, outgoing)
+    exchange_fill(0, tn(hot_rows(gsend_row[...], grid_rows), grid[...]))
     copies[EEI].wait()
     copies[MESH].wait()
     eei = vm[EEI]
@@ -196,34 +214,62 @@
         table_proc[nodes + halo:split_proc, :] = jnp.zeros((split_proc - nodes - halo, lat), BF16)
     if total_proc > split_proc + nodes:
         table_proc[split_proc + nodes:total_proc, :] = jnp.zeros((total_proc - split_proc - nodes, lat), BF16)
+    table_enc[grid_rows:grid_rows + halo, :] = jnp.zeros((halo, lat), BF16)
+    pl.semaphore_wait(barrier, n - 1)
+    exchange_start(0)
     copies[G2M].wait()
+
+    def index_row(ref, t):
+        return ref[pl.ds(t * tile, tile)].reshape(1, tile)
+
+    def encode_local(t):
+        rows = pl.ds(t * tile, tile)
+        pre = nn(hot_pair(index_row(g2m_s, t), index_row(g2m_r, t), split_enc, total_enc), table_enc[...])
+        pre_ref[rows, :] = pre + nn(vm[G2M][rows, :], eei[2 * lat:3 * lat, :])
+
+    for t in range(enc_edges // tile):
+        encode_local(t)
     copies[EEO].wait()
     copies[ENI].wait()
     acc_node[...] = jnp.zeros_like(acc_node)
     upd_ref[...] = nn(mesh[...], vm[ENI][0:lat, :])
+
+    def hot_halo(senders, first, rows_local):
+        held = over_lanes(senders)
+        ids = lax.broadcasted_iota(jnp.int32, (tile, LANE), 1).astype(F32)
+        blocks = [jnp.where(held == ids + float(start), 1.0, 0.0).astype(BF16) for start in range(first, rows_local, LANE)]
+        return blocks[0] if len(blocks) == 1 else jnp.concatenate(blocks, axis=1)
+
+    def halo_rows(own_rows, split, arrived_rows):
+        first = own_rows // LANE * LANE
+        parts = [arrived_rows]
+        if own_rows > first:
+            parts = [jnp.zeros((own_rows - first, lat), BF16)] + parts
+        if split > own_rows + halo:
+            parts = parts + [jnp.zeros((split - own_rows - halo, lat), BF16)]
+        return parts[0] if len(parts) == 1 else jnp.concatenate(parts, axis=0)
+
     arrived = exchange_wait(0)
-    table_enc[grid_rows:grid_rows + halo, :] = nn(arrived, eei[0:lat, :]).astype(BF16)
-
-    def encode(t, carry):
-        rows = pl.ds(pl.multiple_of(t * tile, tile), tile)
-        receivers = g2m_r[t]
-        pre = nn(hot_pair(g2m_s[t], receivers, split_enc, total_enc), table_enc[...])
-        pre = pre + nn(vm[G2M][rows, :], eei[2 * lat:3 * lat, :])
+    far = halo_rows(grid_rows, split_enc, nn(arrived, eei[0:lat, :]).astype(BF16))
+
+    def encode(t):
+        rows = pl.ds(t * tile, tile)
+        pre = pre_ref[rows, :] + nn(hot_halo(index_row(g2m_s, t), grid_rows // LANE * LANE, split_enc), far)
         hidden = (pre * sigmoid(pre)).astype(BF16)
         z, _ = normalise(nn(hidden, vm[EEO][...]))
         message = (z * gains[0:1, :] + biases[0:1, :]).astype(BF16)
-        acc_node[...] += nn(hot_rows(receivers, nodes), message)
-        return carry
-
-    lax.fori_loop(0, enc_edges // tile, encode, 0)
+        acc_node[...] += nn(hot_rows(index_row(g2m_r, t), nodes), message)
+
+    for t in range(enc_edges // tile):
+        encode(t)
     copies[ENO].wait()
     pre = upd_ref[...] + nn(acc_node[...].astype(BF16), vm[ENI][lat:2 * lat, :])
     hidden = (pre * sigmoid(pre)).astype(BF16)
     z, _ = normalise(nn(hidden, vm[ENO][...]))
     encoded = (mesh[...].astype(F32) + z * gains[1:2, :] + biases[1:2, :]).astype(BF16)
     node_table[0:nodes, :] = encoded
-    ids = lax.broadcasted_iota(jnp.int32, (halo, nodes), 1)
-    exchange_start(1, nn(jnp.where(ids == nsend_col[...], 1.0, 0.0).astype(BF16), encoded))
+    exchange_fill(1, tn(hot_rows(nsend_row[...], nodes), encoded))
+    exchange_start(1)
 
     copies[PEI].wait()
     copies[EDGE].wait()
@@ -232,28 +278,29 @@
     pei, pni = vm[PEI], vm[PNI]
     table_proc[0:nodes, :] = nn(encoded, pei[0:lat, :]).astype(BF16)
     table_proc[split_proc:split_proc + nodes, :] = nn(encoded, pei[lat:2 * lat, :]).astype(BF16)
+    table_proc[nodes:nodes + halo, :] = jnp.zeros((halo, lat), BF16)
+    count = count_ref[0]
+
+    def live_rows(ref, t):
+        slot = lax.broadcasted_iota(jnp.int32, (1, tile), 1) + t * tile
+        return jnp.where(slot < count, ref[t], -1)
+
+    def process_local(t):
+        rows = pl.ds(t * tile, tile)
+        pre = nn(hot_pair(live_rows(edge_s, t), live_rows(edge_r, t), split_proc, total_proc), table_proc[...])
+        pre_ref[rows, :] = pre + nn(vm[EDGE][rows, :], pei[2 * lat:3 * lat, :])
+
+    for t in range(slots_total // tile):
+        process_local(t)
     upd_ref[...] = nn(encoded, pni[0:lat, :])
-
-    def edge_part(t, carry):
-        rows = pl.ds(pl.multiple_of(t * tile, tile), tile)
-        pre_ref[rows, :] = nn(vm[EDGE][rows, :], pei[2 * lat:3 * lat, :])
-        return carry
-
-    lax.fori_loop(0, slots_total // tile, edge_part, 0)
     acc_node[...] = jnp.zeros_like(acc_node)
     arrived = exchange_wait(1)
     node_table[nodes:nodes + halo, :] = arrived
-    table_proc[nodes:nodes + halo, :] = nn(arrived, pei[0:lat, :]).astype(BF16)
-    count = count_ref[0]
-
-    def live_rows(ref, t):
-        slot = lax.broadcasted_iota(jnp.int32, (1, tile), 1) + t * tile
-        return jnp.where(slot < count, ref[t], -1)
-
-    def process(t, carry):
-        rows = pl.ds(pl.multiple_of(t * tile, tile), tile)
-        receivers = live_rows(edge_r, t)
-        pre = pre_ref[rows, :] + nn(hot_pair(live_rows(edge_s, t), receivers, split_proc, total_proc), table_proc[...])
+    far = halo_rows(nodes, split_proc, nn(arrived, pei[0:lat, :]).astype(BF16))
+
+    def process(t):
+        rows = pl.ds(t * tile, tile)
+        pre = pre_ref[rows, :] + nn(hot_halo(live_rows(edge_s, t), nodes // LANE * LANE, split_proc), far)
         pre_ref[rows, :] = pre
         hidden = (pre * sigmoid(pre)).astype(BF16)
         hid_ref[rows, :] = hidden
@@ -261,10 +308,10 @@
         z_ref[rows, :] = z
         inv_ref[rows, :] = jnp.broadcast_to(inverse, (tile, LANE))
         message = (z * gains[2:3, :] + biases[2:3, :]).astype(BF16)
-        acc_node[...] += nn(hot_rows(receivers, nodes), message)
-        return carry
-
-    lax.fori_loop(0, slots_total // tile, process, 0)
+        acc_node[...] += nn(hot_rows(live_rows(edge_r, t), nodes), message)
+
+    for t in range(slots_total // tile):
+        process(t)
 
     proc_sum = acc_node[...].astype(BF16)
     copies[PNO].wait()
@@ -275,11 +322,12 @@
     z, inverse = normalise(nn(hidden, pno[...]))
     mesh_out_ref[...] = (encoded.astype(F32) + z * gains[3:4, :] + biases[3:4, :]).astype(BF16)
     lin_grad = norm_back(z, inverse, cot[...].astype(F32) * gains[3:4, :]).astype(BF16)
+    full_ref[0, :, :] = tn(lin_grad, hidden)
+    reduce_step(N0, 0)
     pre_grad = (nt(lin_grad, pno[...]) * silu_slope(pre)).astype(BF16)
-    full_ref[0, :, :] = tn(lin_grad, hidden)
     full_ref[1, :, :] = tn(pre_grad, encoded)
     full_ref[2, :, :] = tn(pre_grad, proc_sum)
-    reduce_step(NODE, 0)
+    reduce_step(N12, 0)
     sum_grad = nt(pre_grad, pni[lat:2 * lat, :]).astype(BF16)
     grad_mesh_ref[...] = cot[...].astype(F32) + nt(pre_grad, pni[0:lat, :])
     if split_proc + nodes < total_proc:
@@ -287,8 +335,8 @@
     table_proc[split_proc:split_proc + nodes, :] = sum_grad
     sum_ref[...] = jnp.zeros_like(sum_ref)
 
-    def edge_back(t, carry):
-        rows = pl.ds(pl.multiple_of(t * tile, tile), tile)
+    def edge_back(t):
+        rows = pl.ds(t * tile, tile)
         senders, receivers = live_rows(edge_s, t), live_rows(edge_r, t)
         held = over_lanes(receivers)
         ids = lax.broadcasted_iota(jnp.int32, (tile, LANE), 1).astype(F32)
@@ -301,42 +349,51 @@
         epg_ref[rows, :] = grad
         sum_ref[0:split_proc, :] += nn(hot_rows(senders, split_proc), grad)
         sum_ref[split_proc:split_proc + nodes, :] += nn(hot_rows(receivers, nodes), grad)
-        return carry
-
-    half = slots_total // tile // 2
-    lax.fori_loop(0, half, edge_back, 0)
-    reduce_step(NODE, 1)
-    lax.fori_loop(half, slots_total // tile, edge_back, 0)
-    reduce_step(NODE, 2)
+
+    for t in range(slots_total // tile):
+        edge_back(t)
+        if t == 0:
+            reduce_step(N0, 1)
+            reduce_step(N12, 1)
     by_sender = sum_ref[0:nodes + halo, :].astype(BF16)
     by_receiver = sum_ref[split_proc:split_proc + nodes, :].astype(BF16)
-    exchange_start(2, nt(by_sender[nodes:nodes + halo, :], pei[0:lat, :]))
+    exchange_fill(2, nt(by_sender[nodes:nodes + halo, :], pei[0:lat, :]))
+    exchange_start(2)
     full_ref[3, :, :] = tn(elg_ref[...], hid_ref[...])
     reduce_step(EOUT, 0)
+    full_ref[5, :, :] = tn(by_receiver, node_table[0:nodes, :])
+    reduce_step(E5, 0)
+    reduce_step(N0, 2)
     full_ref[6, :, :] = tn(epg_ref[...], vm[EDGE][...])
-    reduce_step(EA, 0)
-    reduce_step(NODE, 3)
+    reduce_step(E6, 0)
     reduce_step(EOUT, 1)
+    reduce_step(E5, 1)
     full_ref[4, :, :] = tn(by_sender, node_table[...])
-    full_ref[5, :, :] = tn(by_receiver, node_table[0:nodes, :])
-    reduce_step(EB, 0)
-    reduce_step(EA, 1)
+    reduce_step(E4, 0)
+    reduce_step(N12, 2)
+    reduce_step(E6, 1)
+    reduce_step(N0, 3)
     grad_mesh_ref[...] += nt(by_sender[0:nodes, :], pei[0:lat, :]) + nt(by_receiver, pei[lat:2 * lat, :])
-    reduce_step(EB, 1)
-    reduce_step(EOUT, 2)
+    reduce_step(E4, 1)
     arrived = exchange_wait(2)
     grad_mesh_ref[...] += nn(hot_rows(nsend_row[...], nodes), arrived)
-    reduce_step(NODE, 4)
-    reduce_step(EA, 2)
+    reduce_step(N0, 4)
+    reduce_step(EOUT, 2)
+    reduce_step(E5, 2)
+    reduce_step(N12, 3)
+    reduce_step(E6, 2)
     reduce_step(EOUT, 3)
-    reduce_step(EB, 2)
-    reduce_step(EA, 3)
+    reduce_step(E5, 3)
+    reduce_step(N12, 4)
+    reduce_step(E4, 2)
     reduce_step(EOUT, 4)
-    reduce_step(EB, 3)
-    reduce_step(EA, 4)
-    reduce_step(EB, 4)
-    if inside:
-        for units in (NODE, EOUT, EA, EB):
+    reduce_step(E6, 3)
+    reduce_step(E5, 4)
+    reduce_step(E4, 3)
+    reduce_step(E6, 4)
+    reduce_step(E4, 4)
+    if inside:
+        for units in (N0, N12, EOUT, E4, E5, E6):
             for k in range(stages):
                 remote(units, k).wait_send()
 
@@ -359,8 +416,7 @@
     stages = n.bit_length() - 1
     large = [grid_latent, mesh_latent, g2m_latent, edge_latent, cotangent, *weights]
     small = [
-        grid_send.reshape(halo, 1), node_send.reshape(halo, 1), node_send,
-        g2m_sender.reshape(-1, 1, tile), g2m_receiver.reshape(-1, 1, tile),
+        grid_send, node_send, g2m_sender, g2m_receiver,
         edge_sender.reshape(-1, 1, tile), edge_receiver.reshape(-1, 1, tile), gains, biases,
     ]
     in_vmem = pl.BlockSpec(memory_space=pltpu.VMEM)
@@ -389,20 +445,25 @@
         for dtype in (F32, BF16, BF16):
             scratch += [pltpu.VMEM((UNITS, lat >> (k + 1), lat), dtype) for k in range(stages)]
         scratch += [pltpu.SemaphoreType.DMA((UNITS, stages)), pltpu.SemaphoreType.DMA((UNITS, stages))]
-    mesh_out, grad_mesh, grads = pl.pallas_call(
+    if inside:
+        grad_shapes = [jax.ShapeDtypeStruct((lat // n, width * lat), F32) for width in (3, 1, 2, 1)]
+    else:
+        grad_shapes = [jax.ShapeDtypeStruct((UNITS, lat, lat), F32)]
+    mesh_out, grad_mesh, *grads = pl.pallas_call(
         functools.partial(kernel, n, inside, sizes),
         out_shape=(
             jax.ShapeDtypeStruct((nodes, lat), BF16),
             jax.ShapeDtypeStruct((nodes, lat), F32),
-            jax.ShapeDtypeStruct((UNITS, lat // n if inside else lat, lat), F32),
+            *grad_shapes,
         ),
         in_specs=[pl.BlockSpec(memory_space=pl.ANY)] * 13 + [pl.BlockSpec(memory_space=pltpu.SMEM)] + [in_vmem] * len(small),
-        out_specs=(in_vmem, in_vmem, in_vmem),
+        out_specs=(in_vmem,) * (2 + len(grad_shapes)),
         scratch_shapes=scratch,
         compiler_params=pltpu.CompilerParams(collective_id=0, has_side_effects=True, vmem_limit_bytes=60 * 1024 * 1024),
     )(*large, edge_count, *small)
-    if not inside:
-        grads = lax.psum_scatter(grads, "band", scatter_dimension=1, tiled=True)
+    if inside:
+        return (mesh_out, grad_mesh, *(jnp.transpose(g) for g in grads))
+    grads = lax.psum_scatter(grads[0], "band", scatter_dimension=1, tiled=True)
     edge_scale = 1.0 / (slots_total * n) ** 0.5
     node_scale = 1.0 / (nodes * n) ** 0.5
 

time: 81.5 us -> 65.5 us (0.80)
  Pallas kernels: 68.3 us -> 57.6 us
  other arithmetic: 3.47 us -> 0 us
  local copies, waits for them, and re-layouts: 8.15 us -> 6.35 us
    pallas_call x1, Pallas kernels: 68.3 us -> 57.6 us  [on_device(): pl.pallas_call(functools.partial(kernel, n, inside, sizes), out_shape=(ja...]
    reshape x4 -> x0, local copies, waits for them, and re-layouts: 5.22 us -> none  [the longest x1 1.34 us: on_device(): grid_send.reshape(halo, 1)]
    unnamed x6 -> x14, local copies, waits for them, and re-layouts: 1.57 us -> 6.35 us
    unnamed x2 -> x0, other arithmetic: 1.94 us -> none
    mul x1 -> x0, other arithmetic: 1.53 us -> none  [shard(): jnp.transpose(grads[first:first + count], (0, 2, 1))]
    mul x2 -> x0, local copies, waits for them, and re-layouts: 1.36 us -> none  [shard(): jnp.transpose(grads[first:first + count], (0, 2, 1))]
where the time goes in v2:
time: 65.5 us; the launch traced here: 65.3 us
  Pallas kernels  57.6 us (88%)
  local copies, waits for them, and re-layouts  6.35 us (10%)
  between operations  1.33 us (2%)
    pallas_call x1, Pallas kernels, on_device(): pl.pallas_call(functools.partial(kernel, n, inside, sizes), out_shape=(ja...  57.6 us
    unnamed x14, local copies, waits for them, and re-layouts  6.35 us

profile of v2, /device:TPU:0, one launch (start us, length us, event | category | flops | bytes accessed | tf_op | source)
XLA Modules:
  0.0 65.3 jit_solution(6817673487877186863)
XLA Ops:
  1.3 57.6 %shard_map.253 = (bf16[320,512]{1,0:T(8,128)(2,1)}, f32[320,512]{1,0:T(8,128)}, f32[32,1536]{1,0:T(8,128)}, f32[32,512]{1,0:T(8,128)}, f32[32,1024]{1,0:T(8,128)}, /*index=5*/f32[32,512]{1,0:T(8,128)}) custom-call(bf16[512,512]{1,0:T(8,128)(2,1)} %refs_0_.1, bf16[320,512]{1,0:T(8,128)(2,1)} %refs_1_.1, bf16[768,512]{1,0:T(8,128)(2,1)} %refs_2_.1, ...), custom_call_target="tpu_custom_call" | custom-call | tf_op jit(solution)/shard_map/pallas_call | solution.py:452
  58.9 0.0 copy-start
  58.9 0.0 copy-start.3
  58.9 0.0 copy-start.1
  58.9 0.0 copy-start.2
  58.9 1.8 %copy.35 = bf16[320,512]{1,0:T(8,128)(2,1)} copy(bf16[320,512]{1,0:T(8,128)(2,1)} %get-tuple-element.24) | data formatting | bytes 655360
  60.7 2.0 %copy.36 = f32[320,512]{1,0:T(8,128)} copy(f32[320,512]{1,0:T(8,128)} %get-tuple-element.25) | data formatting | bytes 1310720
  62.7 0.0 copy-done
  62.7 0.7 %copy.37 = f32[1536,32]{0,1:T(8,128)} copy(f32[1536,32]{0,1:T(8,128)S(1)} %bitcast.6) | data formatting | bytes 393216
  63.3 0.0 copy-done.3
  63.3 0.6 copy.38
  64.0 0.0 copy-done.1
  64.0 0.7 %copy.39 = f32[1024,32]{0,1:T(8,128)} copy(f32[1024,32]{0,1:T(8,128)S(1)} %bitcast.7) | data formatting | bytes 262144
  64.6 0.0 copy-done.2
  64.6 0.6 copy.40
Async XLA Ops:
  58.9 3.8 %copy-start = (f32[32,1536]{1,0:T(8,128)S(1)}, f32[32,1536]{1,0:T(8,128)}, u32[]{:S(2)}) copy-start(f32[32,1536]{1,0:T(8,128)} %get-tuple-element.14) | copy-start | bytes 589828
  58.9 4.5 %copy-start.3 = (f32[32,512]{1,0:T(8,128)S(1)}, f32[32,512]{1,0:T(8,128)}, u32[]{:S(2)}) copy-start(f32[32,512]{1,0:T(8,128)} %get-tuple-element.15) | copy-start | bytes 196612
  58.9 5.1 %copy-start.1 = (f32[32,1024]{1,0:T(8,128)S(1)}, f32[32,1024]{1,0:T(8,128)}, u32[]{:S(2)}) copy-start(f32[32,1024]{1,0:T(8,128)} %get-tuple-element.16) | copy-start | bytes 393220
  58.9 5.7 %copy-start.2 = (f32[32,512]{1,0:T(8,128)S(1)}, f32[32,512]{1,0:T(8,128)}, u32[]{:S(2)}) copy-start(f32[32,512]{1,0:T(8,128)} %get-tuple-element.17) | copy-start | bytes 196612
